TPU v7x, 1024 devices: a whole 4x4x32 slice. The times are simulated.
1024 devices in a mesh: dp: 8 (over x, y_lo), wide: 32 (over z), narrow: 4 (over y_hi, core).
Axes of the slice: x: 4, y: 4 (y_hi: 2, y_lo: 2; y = y_hi * 2 + y_lo), z: 32, core: 2. Of those that a mesh axis runs over, the one named last changes fastest.
Arguments:
- grad_parts: bfloat16 [32, 256, 73728], P(('dp', 'narrow'), 'wide'), may hold values from -8 to 8
- weight: bfloat16 [256, 73728], P('wide', ('dp', 'narrow')), may hold values from -12 to 12
- row_state: float32 [256], P('wide'), may hold values from 0.01 to 1
- col_state: float32 [73728], P(('dp', 'narrow')), may hold values from 0.01 to 1
Outputs:
- update: float32 [256, 73728], P('wide', ('dp', 'narrow'))
- new_row_state: float32 [256], P('wide')
- new_col_state: float32 [73728], P(('dp', 'narrow'))
All inputs are finite; a program needn't handle non-finite values.
Results may differ from a plain program's by a relative error of at most 0.0003.
Values sent between devices are 32-bit elements; how exact they have to be, the bound alone decides.
A program may use at most 32 MiB of HBM per device.

v0:
```python
import jax
import jax.numpy as jnp
from jax import lax
from jax.sharding import PartitionSpec as P

FF = 73728
STEP = 100


def on_device(grad_parts, weight, row_state, col_state):
    local_part = grad_parts[0].astype(jnp.float32)
    grad = lax.psum_scatter(local_part, ("dp", "narrow"), scatter_dimension=1, tiled=True)
    rows_all = grad.shape[0] * lax.axis_size("wide")
    square = grad * grad + 1e-30
    col_part = jnp.sum(square, axis=0)
    row_part = jnp.sum(square, axis=1)
    weight_f = weight.astype(jnp.float32)
    weight_part = jnp.sum(weight_f * weight_f)
    col_sum = lax.psum(col_part, "wide")
    row_sum = lax.psum(row_part, ("dp", "narrow"))
    weight_total = lax.psum(weight_part, ("dp", "wide", "narrow"))
    beta = 1.0 - STEP ** (-0.8)
    new_row_state = beta * row_state + (1.0 - beta) * (row_sum / FF)
    new_col_state = beta * col_state + (1.0 - beta) * (col_sum / rows_all)
    factor = new_row_state[:, None] * new_col_state[None, :]
    scaled = grad / jnp.sqrt(factor)
    update_sum = lax.psum(jnp.sum(scaled * scaled), ("dp", "wide", "narrow"))
    clip = jnp.maximum(1.0, jnp.sqrt(update_sum / (rows_all * FF)))
    weight_rms = jnp.maximum(0.001, jnp.sqrt(weight_total / (rows_all * FF)))
    update = weight_rms * scaled / clip
    return (update, new_row_state, new_col_state)


def solution(mesh):
    return jax.shard_map(
        on_device,
        mesh=mesh,
        in_specs=(
            P(("dp", "narrow"), "wide", None),
            P("wide", ("dp", "narrow")),
            P("wide"),
            P(("dp", "narrow")),
        ),
        out_specs=(P("wide", ("dp", "narrow")), P("wide"), P(("dp", "narrow"))),
        check_vma=False,
    )
```

profile of v0, /device:TPU:1, one launch (start us, length us, event | category | flops | bytes accessed | tf_op | source)
XLA Modules:
  0.0 510.0 jit_solution(10399370743785812805)
XLA Ops:
  7.2 0.0 copy-start.1
  7.2 0.0 copy-start.2
  7.2 0.0 copy-start.4
  7.2 0.0 reduce-scatter.2.cloned.1.call-start
  7.2 2.8 bitcast_convert_fusion
  10.1 0.0 reduce-scatter.2.cloned.1.call-update
  10.1 0.0 copy-done.1
  10.1 0.6 multiply_reduce_fusion.1
  10.7 160.0 %reduce-scatter.2.cloned.1.call-done = f32[8,2304]{1,0:T(8,128)} async-done(((f32[8,73728]{1,0:T(8,128)}), f32[8,2304]{1,0:T(8,128)}) %reduce-scatter.2.cloned.1.call-update) | async-done | bytes 73744 | tf_op jit(solution)/shard_map/reduce_scatter | solution.py:12
  170.7 1.0 fusion.1
  171.8 80.7 %psum.30 = f32[2304]{0:T(1024)S(1)} all-reduce(f32[2304]{0:T(1024)S(1)} %get-tuple-element.4), channel_id=1, replica_groups=mesh['dp'=8,'wide'=32,'narrow'=4] {'wide'}, use_global_device_ids=true, to_apply=%region_6.0 | all-reduce | flops 2304 | bytes 18432 | tf_op jit(solution)/shard_map/psum | solution.py:19
  252.5 94.1 %psum.29 = f32[8]{0:T(128)S(1)} all-reduce(f32[8]{0:T(128)S(1)} %get-tuple-element.3), channel_id=1, replica_groups=mesh['dp'=8,'wide'=32,'narrow'=4] {'dp','narrow'}, use_global_device_ids=true, to_apply=%region_4.0 | all-reduce | flops 8 | bytes 64 | tf_op jit(solution)/shard_map/psum | solution.py:20
  346.6 0.0 copy-done.2
  346.6 0.0 copy-done.4
  346.6 0.0 copy-start
  346.7 0.0 copy-start.3
  346.7 1.6 multiply_reduce_fusion
  348.3 152.0 %all-reduce = (f32[]{:T(128)}, f32[]{:T(128)}) all-reduce(f32[]{:T(128)} %multiply_reduce_fusion, f32[]{:T(128)} %multiply_reduce_fusion.1), channel_id=1, replica_groups=mesh['dp'=8,'wide'=32,'narrow'=4] {'dp','wide','narrow'}, use_global_device_ids=true, to_apply=%region_8.0 | all-reduce | flops 2 | bytes 16 | tf_op jit(solution)/shard_map/psum | solution.py:27
  501.5 1.6 multiply_divide_fusion
  503.1 0.0 copy-done
  503.1 0.0 copy-done.3
  (2 shorter events, 0.0 us)
Async XLA Ops:
  7.2 2.9 copy-start.1
  7.2 339.4 %copy-start.2 = (f32[2304]{0:T(1024)S(1)}, f32[2304]{0:T(1024)}, u32[]{:S(2)}) copy-start(f32[2304]{0:T(1024)} %param.7) | copy-start | bytes 27652
  7.2 339.4 %copy-start.4 = (f32[8]{0:T(128)S(1)}, f32[8]{0:T(128)}, u32[]{:S(2)}) copy-start(f32[8]{0:T(128)} %param.6) | copy-start | bytes 100
  7.2 163.5 %reduce-scatter.2.cloned.1.call-start = ((), (), s32[]{:S(2)}) async-start(), calls=%async_computation.1 | async-start | bytes 2433024 | tf_op jit(solution)/shard_map/reduce_scatter | solution.py:12
  346.6 156.5 %copy-start = (f32[2304]{0:T(1024)}, f32[2304]{0:T(1024)S(1)}, u32[]{:S(2)}) copy-start(f32[2304]{0:T(1024)S(1)} %multiply_add_fusion.1) | copy-start | bytes 27652
  346.7 156.5 %copy-start.3 = (f32[8]{0:T(128)}, f32[8]{0:T(128)S(1)}, u32[]{:S(2)}) copy-start(f32[8]{0:T(128)S(1)} %multiply_add_fusion.2) | copy-start | bytes 100
Sparse Core Ops, SparseCore 0:
  11.4 159.2 reduce-scatter.1
where the time goes:
time: 510 us
  blocking collectives  327 us (64%)
  waiting for transfers between devices  160 us (31%)
  between operations  15.4 us (3%)
  other arithmetic  7.67 us (2%)
    reduce_scatter x1, waiting for transfers between devices, on_device(): lax.psum_scatter(local_part, ('dp', 'narrow'), scatter_dimension=1, tiled...  160 us
    psum x1, blocking collectives, on_device(): update_sum = lax.psum(jnp.sum(scaled * scaled), ('dp', 'wide', 'narrow'))  152 us
    psum x1, blocking collectives, on_device(): row_sum = lax.psum(row_part, ('dp', 'narrow'))  94.1 us
    psum x1, blocking collectives, on_device(): col_sum = lax.psum(col_part, 'wide')  80.7 us
  transfers between devices with their start and end apart: 1, of which 1 were waited for; matrix products, arithmetic and copies ran while one was open for 0% of the time, Pallas kernels for 0%

commit v1 on v0

v1 whole, which is shorter than its diff:
```python
import functools

import jax
import jax.numpy as jnp
from jax import lax
from jax.experimental import pallas as pl
from jax.experimental.pallas import tpu as pltpu
from jax.sharding import PartitionSpec as P

FF = 73728
ROWS = 256
STEP = 100
BETA = 1.0 - STEP ** (-0.8)

MESH = pl.DeviceIdType.MESH
F32 = jnp.float32
R = 8
OWN = 2304
HALF = OWN // 2
GROUPS = OWN // 128
PLANE = 32
Z = 32
CUT = 640

ORDER = ((0, 2), (1, 2), (0, 1), (0, 3), (1, 1), (1, 3), (0, 0), (1, 0))


def chip(x, y, z, c):
    return (x * 2 + y % 2, z, (y // 2) * 2 + c)


def kernel(
    g_hbm, w_ref, row_ref, col_ref,
    upd_ref, nrow_ref, ncol_ref,
    gbuf, part, pair, acc, r1, r2, red, s1, s2, grad,
    wsrc, wz, rsrc, rz, zsrc, zr, zg, tsrc, tz,
    load_sem, p_send, p_recv, a_send, a_recv, b_send, b_recv,
    w_send, w_recv, r_send, r_recv, c_send, c_recv, ag_send, ag_recv, t_send, t_recv,
):
    dp = lax.axis_index("dp")
    z = lax.axis_index("wide")
    nr = lax.axis_index("narrow")
    x, y, core = dp // 2, (nr // 2) * 2 + dp % 2, nr % 2
    me = dp * 4 + nr

    load = pltpu.make_async_copy(g_hbm.at[0], gbuf, load_sem)
    load.start()

    def plane_peer(j):
        t = (me + j) % PLANE
        return (t // 4, z, t % 4)

    def z_peer(j):
        return (dp, (z + j) % Z, nr)

    barrier = pltpu.get_barrier_semaphore()

    @pl.loop(1, PLANE)
    def _(j):
        pl.semaphore_signal(barrier, inc=1, device_id=plane_peer(j), device_id_type=MESH)
        pl.semaphore_signal(barrier, inc=1, device_id=z_peer(j), device_id_type=MESH)

    wacc = jnp.zeros((R, 128), F32)
    for k in range(GROUPS):
        wk = w_ref[:, k * 128:(k + 1) * 128].astype(F32)
        wacc = wacc + wk * wk
    wsrc[...] = jnp.sum(wacc, axis=0, keepdims=True)
    load.wait()
    pl.semaphore_wait(barrier, PLANE - 1 + Z - 1)

    def cols(h, d, e, c):
        tx = (x + (d if h == 0 else e)) % 4
        ty = (y + (e if h == 0 else d)) % 4
        owner = ((tx * 2 + ty % 2) * 2 + ty // 2) * 2 + c
        return pl.ds(pl.multiple_of(owner * OWN + h * HALF, 128), HALF)

    other = chip(x, y, z, 1 - core)
    swaps = []
    for i, (h, d) in enumerate(ORDER):
        @pl.loop(0, 4)
        def _(e):
            part[h, d, e] = gbuf[:, cols(h, d, e, 1 - core)].astype(F32)

        copy = pltpu.make_async_remote_copy(
            part.at[h, d], pair.at[h, d], p_send.at[i], p_recv.at[i], other, MESH)
        copy.start()
        swaps.append(copy)

    def near(axis, s):
        if axis == 0:
            return chip((x + 4 + s) % 4, y, z, core)
        return chip(x, (y + 4 + s) % 4, z, core)

    def remote(src, dst, sems, i, device):
        return pltpu.make_async_remote_copy(
            src, dst, sems[0].at[i], sems[1].at[i], device, MESH)

    first = [[None] * 6, [None] * 6]
    for h in range(2):
        sems = (a_send.at[h], a_recv.at[h])
        up, down = near(h, 1), near(h, -1)
        first[h][0] = remote(acc.at[h, 2, pl.ds(0, 2)], r1.at[h, 0], sems, 0, up)
        first[h][1] = remote(acc.at[h, 2, pl.ds(2, 2)], r1.at[h, 1], sems, 1, down)
        first[h][2] = remote(acc.at[h, 1, pl.ds(2, 2)], r2.at[h, 0, pl.ds(2, 2)], sems, 2, up)
        first[h][3] = remote(acc.at[h, 3, pl.ds(0, 2)], r2.at[h, 1, pl.ds(0, 2)], sems, 3, down)
        first[h][4] = remote(acc.at[h, 1, pl.ds(0, 2)], r2.at[h, 0, pl.ds(0, 2)], sems, 4, up)
        first[h][5] = remote(acc.at[h, 3, pl.ds(2, 2)], r2.at[h, 1, pl.ds(2, 2)], sems, 5, down)

    for i, (h, d) in enumerate(ORDER):
        swaps[i].wait_recv()

        @pl.loop(0, 4)
        def _(e):
            acc[h, d, e] = gbuf[:, cols(h, d, e, core)].astype(F32) + pair[h, d, e]

        if d == 2:
            first[h][0].start()
            first[h][1].start()
        elif d == 1:
            first[h][2].start()
        elif d == 3:
            first[h][3].start()

    @pl.loop(1, Z)
    def _(j):
        pltpu.make_async_remote_copy(
            wsrc, wz.at[j - 1], w_send, w_recv, z_peer(j), MESH).start()

    for h in range(2):
        first[h][0].wait_recv()
        for e in range(2):
            acc[h, 1, e] = acc[h, 1, e] + r1[h, 0, e]
        first[h][4].start()
        first[h][1].wait_recv()
        for e in range(2):
            acc[h, 3, 2 + e] = acc[h, 3, 2 + e] + r1[h, 1, e]
        first[h][5].start()

    second = [[None] * 6, [None] * 6]
    lo, hi = pl.ds(0, CUT), pl.ds(CUT, HALF - CUT)
    for h in range(2):
        sems = (b_send.at[h], b_recv.at[h])
        up, down = near(1 - h, 1), near(1 - h, -1)
        second[h][0] = remote(red.at[h, 2, :, lo], s1.at[h, :, lo], sems, 0, up)
        second[h][1] = remote(red.at[h, 2, :, hi], s1.at[h, :, hi], sems, 1, down)
        second[h][2] = remote(red.at[h, 1, :, hi], s2.at[h, 0, :, hi], sems, 2, up)
        second[h][3] = remote(red.at[h, 3, :, lo], s2.at[h, 1, :, lo], sems, 3, down)
        second[h][4] = remote(red.at[h, 1, :, lo], s2.at[h, 0, :, lo], sems, 4, up)
        second[h][5] = remote(red.at[h, 3, :, hi], s2.at[h, 1, :, hi], sems, 5, down)

    for h in range(2):
        for i in range(2, 6):
            first[h][i].wait_recv()
        for e in (2, 1, 3, 0):
            red[h, e] = acc[h, 0, e] + r2[h, 0, e] + r2[h, 1, e]
            if e == 2:
                second[h][0].start()
                second[h][1].start()
            elif e == 1:
                second[h][2].start()
            elif e == 3:
                second[h][3].start()
    for h in range(2):
        second[h][0].wait_recv()
        red[h, 1, :, lo] = red[h, 1, :, lo] + s1[h, :, lo]
        second[h][4].start()
        second[h][1].wait_recv()
        red[h, 3, :, hi] = red[h, 3, :, hi] + s1[h, :, hi]
        second[h][5].start()

    rowacc = jnp.zeros((R, 128), F32)
    for h in range(2):
        for i in range(2, 6):
            second[h][i].wait_recv()
        for k in range(HALF // 128):
            at = pl.ds(k * 128, 128)
            g = red[h, 0, :, at] + s2[h, 0, :, at] + s2[h, 1, :, at]
            grad[:, h * HALF + k * 128:h * HALF + (k + 1) * 128] = g
            rowacc = rowacc + (g * g + 1e-30)

    diagonal = (lax.broadcasted_iota(jnp.int32, (R, 128), 0)
                == lax.broadcasted_iota(jnp.int32, (R, 128), 1))
    rowsum = jnp.sum(rowacc, axis=1, keepdims=True)
    rsrc[...] = jnp.sum(jnp.where(diagonal, rowsum, 0.0), axis=0, keepdims=True)

    @pl.loop(1, PLANE)
    def _(j):
        pltpu.make_async_remote_copy(
            rsrc, rz.at[j - 1], r_send, r_recv, plane_peer(j), MESH).start()

    def all_of(ref, send, recv):
        return pltpu.make_async_remote_copy(ref, ref, send, recv, other, MESH)

    all_of(rz, r_send, r_recv).wait_recv()
    rowtotal = rsrc[...] + jnp.sum(rz[...], axis=0)
    new_row = BETA * row_ref[...] + (1.0 - BETA) * (rowtotal[:, :R] / FF)
    nrow_ref[...] = new_row
    eye = (lax.broadcasted_iota(jnp.int32, (R, R), 0)
           == lax.broadcasted_iota(jnp.int32, (R, R), 1))
    rows = jnp.sum(jnp.where(eye, jnp.broadcast_to(new_row, (R, R)), 0.0), axis=1, keepdims=True)
    inv_rows = jnp.broadcast_to(1.0 / rows, (R, 128))

    for k in range(GROUPS):
        g = grad[:, k * 128:(k + 1) * 128]
        square = g * g
        zsrc[k, 0:1] = jnp.sum(square + 1e-30, axis=0, keepdims=True)
        zsrc[k, 1:2] = jnp.sum(square * inv_rows, axis=0, keepdims=True)

    mine = (9 * z + 15) // 16
    is_owner = ((16 * mine) // 9 == z) & (mine < GROUPS)

    @pl.loop(0, GROUPS)
    def _(k):
        to = (16 * k) // 9

        @pl.when(to != z)
        def _():
            pltpu.make_async_remote_copy(
                zsrc.at[k], zr.at[(z - to + Z) % Z - 1], c_send, c_recv,
                (dp, to, nr), MESH).start()

    @pl.when(is_owner)
    def _():
        all_of(zr, c_send, c_recv).wait_recv()
        own = zsrc[mine] + jnp.sum(zr[...], axis=0)
        col = col_ref[pl.ds(mine, 1), :]
        new_col = BETA * col + (1.0 - BETA) * (own[0:1] / ROWS)
        zg[mine, 0:1] = new_col
        zg[mine, 1:2] = own[1:2] / new_col

        @pl.loop(1, Z)
        def _(j):
            pltpu.make_async_remote_copy(
                zg.at[mine], zg.at[mine], ag_send, ag_recv.at[mine],
                z_peer(j), MESH).start()

    all_of(wz, w_send, w_recv).wait_recv()
    tsrc[1:2] = wsrc[...] + jnp.sum(wz[...], axis=0)
    inv_sqrt_rows = jnp.broadcast_to(lax.rsqrt(rows), (R, 128))

    @pl.loop(0, GROUPS)
    def _(k):
        @pl.when((16 * k) // 9 != z)
        def _():
            pltpu.make_async_remote_copy(
                zg.at[k], zg.at[k], ag_send, ag_recv.at[k], other, MESH).wait_recv()

    tsrc[0:1] = jnp.sum(zg[...], axis=0)[1:2]

    @pl.loop(1, PLANE)
    def _(j):
        pltpu.make_async_remote_copy(
            tsrc, tz.at[j - 1], t_send, t_recv, plane_peer(j), MESH).start()

    for k in range(GROUPS):
        new_col = zg[k, 0:1]
        ncol_ref[k:k + 1] = new_col
        at = slice(k * 128, (k + 1) * 128)
        grad[:, at] = grad[:, at] * inv_sqrt_rows * lax.rsqrt(new_col)

    all_of(tz, t_send, t_recv).wait_recv()
    total = jnp.sum(tsrc[...] + jnp.sum(tz[...], axis=0), axis=1, keepdims=True)
    root = jnp.sqrt(total / (ROWS * FF))
    clip = jnp.maximum(1.0, root[0:1])
    weight_rms = jnp.maximum(0.001, root[1:2])
    upd_ref[...] = grad[...] * (weight_rms / clip)

    for i in range(8):
        swaps[i].wait_send()
    for h in range(2):
        for i in range(6):
            first[h][i].wait_send()
            second[h][i].wait_send()
    all_of(wz, w_send, w_recv).wait_send()
    all_of(rz, r_send, r_recv).wait_send()
    all_of(tz, t_send, t_recv).wait_send()

    @pl.when(is_owner)
    def _():
        all_of(zr.at[pl.ds(0, GROUPS - 1)], c_send, c_recv).wait_send()
        all_of(zr, ag_send, c_recv).wait_send()

    @pl.when(jnp.logical_not(is_owner))
    def _():
        all_of(zr.at[pl.ds(0, GROUPS)], c_send, c_recv).wait_send()


def on_device(grad_parts, weight, row_state, col_state):
    vmem = pl.BlockSpec(memory_space=pltpu.VMEM)
    dma = pltpu.SemaphoreType.DMA
    update, new_row, new_col = pl.pallas_call(
        kernel,
        out_shape=(
            jax.ShapeDtypeStruct((R, OWN), F32),
            jax.ShapeDtypeStruct((1, R), F32),
            jax.ShapeDtypeStruct((GROUPS, 128), F32),
        ),
        in_specs=[pl.BlockSpec(memory_space=pltpu.HBM), vmem, vmem, vmem],
        out_specs=(vmem, vmem, vmem),
        scratch_shapes=[
            pltpu.VMEM((R, FF), jnp.bfloat16),
            pltpu.VMEM((2, 4, 4, R, HALF), F32),
            pltpu.VMEM((2, 4, 4, R, HALF), F32),
            pltpu.VMEM((2, 4, 4, R, HALF), F32),
            pltpu.VMEM((2, 2, 2, R, HALF), F32),
            pltpu.VMEM((2, 2, 4, R, HALF), F32),
            pltpu.VMEM((2, 4, R, HALF), F32),
            pltpu.VMEM((2, R, HALF), F32),
            pltpu.VMEM((2, 2, R, HALF), F32),
            pltpu.VMEM((R, OWN), F32),
            pltpu.VMEM((1, 128), F32),
            pltpu.VMEM((Z - 1, 1, 128), F32),
            pltpu.VMEM((1, 128), F32),
            pltpu.VMEM((PLANE - 1, 1, 128), F32),
            pltpu.VMEM((GROUPS, 2, 128), F32),
            pltpu.VMEM((Z - 1, 2, 128), F32),
            pltpu.VMEM((GROUPS, 2, 128), F32),
            pltpu.VMEM((2, 128), F32),
            pltpu.VMEM((PLANE - 1, 2, 128), F32),
            dma,
            dma((8,)), dma((8,)),
            dma((2, 6)), dma((2, 6)),
            dma((2, 6)), dma((2, 6)),
            dma, dma,
            dma, dma,
            dma, dma,
            dma, dma((GROUPS,)),
            dma, dma,
        ],
        compiler_params=pltpu.CompilerParams(
            collective_id=0, has_side_effects=True, vmem_limit_bytes=48 * 2**20
        ),
    )(grad_parts, weight, row_state.reshape(1, R), col_state.reshape(GROUPS, 128))
    return update, new_row.reshape(R), new_col.reshape(OWN)


def solution(mesh):
    return jax.shard_map(
        on_device,
        mesh=mesh,
        in_specs=(
            P(("dp", "narrow"), "wide", None),
            P("wide", ("dp", "narrow")),
            P("wide"),
            P(("dp", "narrow")),
        ),
        out_specs=(P("wide", ("dp", "narrow")), P("wide"), P(("dp", "narrow"))),
        check_vma=False,
    )
```

time: 510 us -> 90.5 us (0.18)
  blocking collectives: 327 us -> 0 us
  waiting for transfers between devices: 160 us -> 0 us
  Pallas kernels: 0 us -> 84.4 us
  between operations: 15.4 us -> 0.65 us
  other arithmetic: 7.67 us -> 0 us
  local copies, waits for them, and re-layouts: 0.03 us -> 5.14 us
    psum x3 -> x0, blocking collectives: 327 us -> none  [the longest x1 152 us: on_device(): update_sum = lax.psum(jnp.sum(scaled * scaled), ('dp', 'wide', 'narrow'))]
    reduce_scatter x1 -> x0, waiting for transfers between devices: 160 us -> none  [on_device(): lax.psum_scatter(local_part, ('dp', 'narrow'), scatter_dimension=1, tiled...]
    pallas_call x0 -> x1, Pallas kernels: none -> 84.4 us  [on_device(): pl.pallas_call(kernel, out_shape=(jax.ShapeDtypeStruct((R, OWN), F32), ja...]
    unnamed x10 -> x11, local copies, waits for them, and re-layouts: 0.03 us -> 5.14 us
  transfers between devices with their start and end apart: 1 -> 0, of which waited for: 1 -> 0; matrix products, arithmetic and copies ran while one was open for 0% -> 0% of each run, Pallas kernels for 0% -> 0%
where the time goes in v1:
time: 90.5 us; the launch traced here: 90.2 us
  Pallas kernels  84.4 us (93%)
  local copies, waits for them, and re-layouts  5.14 us (6%)
    pallas_call x1, Pallas kernels, on_device(): pl.pallas_call(kernel, out_shape=(jax.ShapeDtypeStruct((R, OWN), F32), ja...  84.4 us
    unnamed x11, local copies, waits for them, and re-layouts  5.14 us

profile of v1, /device:TPU:1, one launch (start us, length us, event | category | flops | bytes accessed | tf_op | source)
XLA Modules:
  0.0 90.2 jit_solution(13987139439416096551)
XLA Ops:
  0.6 0.0 copy-start
  0.6 1.3 %copy-done = bf16[1,8,73728]{2,1,0:T(8,128)(2,1)S(1)} copy-done((bf16[1,8,73728]{2,1,0:T(8,128)(2,1)S(1)}, bf16[1,8,73728]{2,1,0:T(8,128)(2,1)}, u32[]{:S(2)}) %copy-start) | copy-done | bytes 1179672
  1.9 0.0 copy-start.1
  1.9 0.8 copy-done.1
  2.7 0.0 copy-start.2
  2.7 0.7 copy-done.2
  3.4 0.0 copy-start.3
  3.4 0.7 copy-done.3
  4.0 84.4 %shard_map.67 = (f32[8,2304]{1,0:T(8,128)S(1)}, f32[1,8]{1,0:T(1,128)S(1)}, f32[18,128]{1,0:T(8,128)S(1)}) custom-call(bf16[1,8,73728]{2,1,0:T(8,128)(2,1)S(1)} %copy-done, bf16[8,2304]{1,0:T(8,128)(2,1)S(1)} %copy-done.1, f32[1,8]{1,0:T(1,128)S(1)} %bitcast.6, f32[18,128]{1,0:T(8,128)S(1)} %bitcast.4), custom_call_target="tpu_custom_call" | custom-call | tf_op jit(solution)/shard_map/pallas_call | solution.py:291
  88.4 0.6 copy.10
  89.1 0.5 copy.11
  89.6 0.6 copy.12
Async XLA Ops:
  0.6 1.3 %copy-start = (bf16[1,8,73728]{2,1,0:T(8,128)(2,1)S(1)}, bf16[1,8,73728]{2,1,0:T(8,128)(2,1)}, u32[]{:S(2)}) copy-start(bf16[1,8,73728]{2,1,0:T(8,128)(2,1)} %g_hbm.1) | copy-start | bytes 3538948
  1.9 0.8 copy-start.1
  2.7 0.7 copy-start.2
  3.4 0.7 copy-start.3

commit v2 on v1

v2 whole, which is shorter than its diff:
```python
import jax
import jax.numpy as jnp
from jax import lax
from jax.experimental import pallas as pl
from jax.experimental.pallas import tpu as pltpu
from jax.sharding import PartitionSpec as P

FF = 73728
ROWS = 256
STEP = 100
BETA = 1.0 - STEP ** (-0.8)

MESH = pl.DeviceIdType.MESH
F32 = jnp.float32
R = 8
OWN = 2304
HALF = OWN // 2
GROUPS = OWN // 128
PLANE = 32
Z = 32
NEAR = 4
CUT = 640

ORDER = ((0, 2), (1, 2), (0, 1), (0, 3), (1, 1), (1, 3), (0, 0), (1, 0))


def chip(x, y, z, c):
    return (x * 2 + y % 2, z, (y // 2) * 2 + c)


def far_first(i, far):
    return far + ((i + 1) // 2) * (2 * ((i + 1) % 2) - 1)


def kernel(
    g_hbm, w_hbm, row_hbm, col_hbm,
    upd_ref, nrow_ref, ncol_ref,
    gbuf, w_ref, row_ref, col_ref, part, pair, acc, r1, r2, red, s1, s2, grad,
    wz, rz, zsrc, zr, zr2, zg, tz,
    load_sem, p_send, p_recv, a_send, a_recv, b_send, b_recv,
    w_send, w_recv, r_send, r_recv, c_send, c_recv, c2_send, c2_recv, ag_send, ag_recv, t_send, t_recv,
    reach4, reach8,
):
    dp = lax.axis_index("dp")
    z = lax.axis_index("wide")
    nr = lax.axis_index("narrow")
    x, y, core = dp // 2, (nr // 2) * 2 + dp % 2, nr % 2
    me = dp * 4 + nr
    other = chip(x, y, z, 1 - core)

    sent = []

    loads = [
        pltpu.make_async_copy(src, dst, load_sem.at[i])
        for i, (src, dst) in enumerate(
            ((g_hbm.at[0], gbuf), (w_hbm, w_ref), (row_hbm, row_ref), (col_hbm, col_ref)))
    ]
    for load in loads:
        load.start()

    def plane_peer(j):
        t = (me + j) % PLANE
        return (t // 4, z, t % 4)

    def z_peer(j):
        return (dp, (z + j) % Z, nr)

    def signal(sem, device):
        pl.semaphore_signal(sem, inc=1, device_id=device, device_id_type=MESH)

    def bytes_of(ref, send, recv):
        return pltpu.make_async_remote_copy(ref, ref, send, recv, other, MESH)

    barrier = pltpu.get_barrier_semaphore()

    @pl.loop(1, PLANE)
    def _(j):
        signal(barrier, plane_peer(j))

    @pl.loop(1, NEAR + 1)
    def _(j):
        signal(barrier, z_peer(j))
        signal(barrier, z_peer(Z - j))

    for load in loads:
        load.wait()

    wacc = jnp.zeros((R, 128), F32)
    for k in range(GROUPS):
        wk = w_ref[:, k * 128:(k + 1) * 128].astype(F32)
        wacc = wacc + wk * wk
    wz[z] = jnp.sum(wacc, axis=0, keepdims=True)

    pl.semaphore_wait(barrier, PLANE - 1 + 2 * NEAR)
    signal(reach4, z_peer(NEAR))
    signal(reach4, z_peer(Z - NEAR))

    def cols(h, d, e, c):
        tx = (x + (d if h == 0 else e)) % 4
        ty = (y + (e if h == 0 else d)) % 4
        owner = ((tx * 2 + ty % 2) * 2 + ty // 2) * 2 + c
        return pl.ds(pl.multiple_of(owner * OWN + h * HALF, 128), HALF)

    swaps = []
    for i, (h, d) in enumerate(ORDER):
        @pl.loop(0, 4)
        def _(e):
            part[h, d, e] = gbuf[:, cols(h, d, e, 1 - core)].astype(F32)

        copy = pltpu.make_async_remote_copy(
            part.at[h, d], pair.at[h, d], p_send.at[i], p_recv.at[i], other, MESH)
        copy.start()
        swaps.append(copy)
        sent.append(copy.wait_send)

    def near(axis, s):
        if axis == 0:
            return chip((x + 4 + s) % 4, y, z, core)
        return chip(x, (y + 4 + s) % 4, z, core)

    def remote(src, dst, sems, i, device):
        return pltpu.make_async_remote_copy(
            src, dst, sems[0].at[i], sems[1].at[i], device, MESH)

    first = [[None] * 6, [None] * 6]
    for h in range(2):
        sems = (a_send.at[h], a_recv.at[h])
        up, down = near(h, 1), near(h, -1)
        first[h][0] = remote(acc.at[h, 2, pl.ds(0, 2)], r1.at[h, 0], sems, 0, up)
        first[h][1] = remote(acc.at[h, 2, pl.ds(2, 2)], r1.at[h, 1], sems, 1, down)
        first[h][2] = remote(acc.at[h, 1, pl.ds(2, 2)], r2.at[h, 0, pl.ds(2, 2)], sems, 2, up)
        first[h][3] = remote(acc.at[h, 3, pl.ds(0, 2)], r2.at[h, 1, pl.ds(0, 2)], sems, 3, down)
        first[h][4] = remote(acc.at[h, 1, pl.ds(0, 2)], r2.at[h, 0, pl.ds(0, 2)], sems, 4, up)
        first[h][5] = remote(acc.at[h, 3, pl.ds(2, 2)], r2.at[h, 1, pl.ds(2, 2)], sems, 5, down)
        sent.extend(copy.wait_send for copy in first[h])

    for i, (h, d) in enumerate(ORDER):
        swaps[i].wait_recv()

        @pl.loop(0, 4)
        def _(e):
            acc[h, d, e] = gbuf[:, cols(h, d, e, core)].astype(F32) + pair[h, d, e]

        if d == 2:
            first[h][0].start()
            first[h][1].start()
        elif d == 1:
            first[h][2].start()
        elif d == 3:
            first[h][3].start()

    pl.semaphore_wait(reach4, 2)
    signal(reach8, z_peer(2 * NEAR))
    signal(reach8, z_peer(Z - 2 * NEAR))

    for h in range(2):
        first[h][0].wait_recv()
        for e in range(2):
            acc[h, 1, e] = acc[h, 1, e] + r1[h, 0, e]
        first[h][4].start()
        first[h][1].wait_recv()
        for e in range(2):
            acc[h, 3, 2 + e] = acc[h, 3, 2 + e] + r1[h, 1, e]
        first[h][5].start()

    second = [[None] * 6, [None] * 6]
    lo, hi = pl.ds(0, CUT), pl.ds(CUT, HALF - CUT)
    for h in range(2):
        sems = (b_send.at[h], b_recv.at[h])
        up, down = near(1 - h, 1), near(1 - h, -1)
        second[h][0] = remote(red.at[h, 2, :, lo], s1.at[h, :, lo], sems, 0, up)
        second[h][1] = remote(red.at[h, 2, :, hi], s1.at[h, :, hi], sems, 1, down)
        second[h][2] = remote(red.at[h, 1, :, hi], s2.at[h, 0, :, hi], sems, 2, up)
        second[h][3] = remote(red.at[h, 3, :, lo], s2.at[h, 1, :, lo], sems, 3, down)
        second[h][4] = remote(red.at[h, 1, :, lo], s2.at[h, 0, :, lo], sems, 4, up)
        second[h][5] = remote(red.at[h, 3, :, hi], s2.at[h, 1, :, hi], sems, 5, down)
        sent.extend(copy.wait_send for copy in second[h])

    for h in range(2):
        for i in range(2, 6):
            first[h][i].wait_recv()
        for e in (2, 1, 3, 0):
            red[h, e] = acc[h, 0, e] + r2[h, 0, e] + r2[h, 1, e]
            if e == 2:
                second[h][0].start()
                second[h][1].start()
            elif e == 1:
                second[h][2].start()
            elif e == 3:
                second[h][3].start()
    for h in range(2):
        second[h][0].wait_recv()
        red[h, 1, :, lo] = red[h, 1, :, lo] + s1[h, :, lo]
        second[h][4].start()
        second[h][1].wait_recv()
        red[h, 3, :, hi] = red[h, 3, :, hi] + s1[h, :, hi]
        second[h][5].start()

    rowacc = jnp.zeros((R, 128), F32)
    for h in range(2):
        for i in range(2, 6):
            second[h][i].wait_recv()
        for k in range(HALF // 128):
            at = pl.ds(k * 128, 128)
            g = red[h, 0, :, at] + s2[h, 0, :, at] + s2[h, 1, :, at]
            grad[:, h * HALF + k * 128:h * HALF + (k + 1) * 128] = g
            rowacc = rowacc + (g * g + 1e-30)

    diagonal = (lax.broadcasted_iota(jnp.int32, (R, 128), 0)
                == lax.broadcasted_iota(jnp.int32, (R, 128), 1))
    rowsum = jnp.sum(rowacc, axis=1, keepdims=True)
    rz[me] = jnp.sum(jnp.where(diagonal, rowsum, 0.0), axis=0, keepdims=True)

    @pl.loop(1, PLANE)
    def _(j):
        pltpu.make_async_remote_copy(
            rz.at[me], rz.at[me], r_send, r_recv, plane_peer(j), MESH).start()

    rest = bytes_of(rz.at[pl.ds(1, PLANE - 1)], r_send, r_recv)
    sent.append(rest.wait_send)
    rest.wait_recv()
    rowtotal = jnp.sum(rz[...], axis=0)
    new_row = BETA * row_ref[...] + (1.0 - BETA) * (rowtotal[:, :R] / FF)
    nrow_ref[...] = new_row
    eye = (lax.broadcasted_iota(jnp.int32, (R, R), 0)
           == lax.broadcasted_iota(jnp.int32, (R, R), 1))
    rows = jnp.sum(jnp.where(eye, jnp.broadcast_to(new_row, (R, R)), 0.0), axis=1, keepdims=True)
    inv_rows = jnp.broadcast_to(1.0 / rows, (R, 128))

    for k in range(GROUPS):
        g = grad[:, k * 128:(k + 1) * 128]
        square = g * g
        zsrc[k, 0:1] = jnp.sum(square + 1e-30, axis=0, keepdims=True)
        zsrc[k, 1:2] = jnp.sum(square * inv_rows, axis=0, keepdims=True)

    pl.semaphore_wait(reach8, 2)

    @pl.loop(0, Z - 1)
    def _(i):
        off = far_first(i, 16)
        pltpu.make_async_remote_copy(
            zsrc.at[(z + off) % 16], zr.at[z], c_send, c_recv, z_peer(off), MESH).start()

    rest_c = bytes_of(zr.at[pl.ds(1, Z - 1)], c_send, c_recv)
    sent.append(rest_c.wait_send)
    twice = z % 8 == 4

    def extra(t):
        return 16 + (t % 16) // 12

    def to_extra(i):
        t = 8 * i + 4
        return t != z, pltpu.make_async_remote_copy(
            zsrc.at[extra(t)], zr2.at[z], c2_send.at[i], c2_recv, (dp, t, nr), MESH)

    @pl.loop(0, 4)
    def _(i):
        needed, copy = to_extra(i)

        @pl.when(needed)
        def _():
            copy.start()

    def sent_extra():
        @pl.loop(0, 4)
        def _(i):
            needed, copy = to_extra(i)

            @pl.when(needed)
            def _():
                copy.wait_send()

    sent.append(sent_extra)

    @pl.loop(0, Z - 1)
    def _(i):
        pltpu.make_async_remote_copy(
            wz.at[z], wz.at[z], w_send, w_recv, z_peer(far_first(i, 16)), MESH).start()

    rest_w = bytes_of(wz.at[pl.ds(1, Z - 1)], w_send, w_recv)
    sent.append(rest_w.wait_send)

    def finish_group(got, k, sem):
        own = jnp.sum(got[...], axis=0)
        new_col = BETA * col_ref[pl.ds(k, 1), :] + (1.0 - BETA) * (own[0:1] / ROWS)
        zg[k, 0:1] = new_col
        zg[k, 1:2] = own[1:2] / new_col

        @pl.loop(0, 15)
        def _(i):
            off = (1 - i % 2) * (Z - 8 + i // 2) + (i % 2) * (7 - i // 2)
            pltpu.make_async_remote_copy(
                zg.at[k], zg.at[k], sem, ag_recv.at[k], z_peer(off), MESH).start()

    def sent_group(sem):
        return bytes_of(zg.at[pl.ds(0, 15)], sem, c_recv).wait_send()

    zr[z] = zsrc[z % 16]
    rest_c.wait_recv()
    finish_group(zr, z % 16, ag_send.at[0])
    sent.append(lambda: sent_group(ag_send.at[0]))

    @pl.when(twice)
    def _():
        zr2[z] = zsrc[extra(z)]
        bytes_of(zr2.at[pl.ds(1, Z - 1)], c_send, c2_recv).wait_recv()
        finish_group(zr2, extra(z), ag_send.at[1])

    def sent_twice():
        @pl.when(twice)
        def _():
            sent_group(ag_send.at[1])

    sent.append(sent_twice)

    inv_sqrt_rows = jnp.broadcast_to(lax.rsqrt(rows), (R, 128))
    for k in range(GROUPS):
        at = slice(k * 128, (k + 1) * 128)
        grad[:, at] = grad[:, at] * inv_sqrt_rows

    @pl.loop(0, GROUPS)
    def _(k):
        local = (k == z % 16) | (twice & (k == extra(z)))

        @pl.when(jnp.logical_not(local))
        def _():
            bytes_of(zg.at[k], c_send, ag_recv.at[k]).wait_recv()

    tz[me, 0:1] = jnp.sum(zg[...], axis=0)[1:2]
    rest_w.wait_recv()
    tz[me, 1:2] = jnp.sum(wz[...], axis=0)

    @pl.loop(1, PLANE)
    def _(j):
        pltpu.make_async_remote_copy(
            tz.at[me], tz.at[me], t_send, t_recv, plane_peer(j), MESH).start()

    rest_t = bytes_of(tz.at[pl.ds(1, PLANE - 1)], t_send, t_recv)
    sent.append(rest_t.wait_send)

    for k in range(GROUPS):
        new_col = zg[k, 0:1]
        ncol_ref[k:k + 1] = new_col
        at = slice(k * 128, (k + 1) * 128)
        grad[:, at] = grad[:, at] * lax.rsqrt(new_col)

    rest_t.wait_recv()
    total = jnp.sum(jnp.sum(tz[...], axis=0), axis=1, keepdims=True)
    root = jnp.sqrt(total / (ROWS * FF))
    clip = jnp.maximum(1.0, root[0:1])
    weight_rms = jnp.maximum(0.001, root[1:2])
    upd_ref[...] = grad[...] * (weight_rms / clip)

    for wait in sent:
        wait()


def on_device(grad_parts, weight, row_state, col_state):
    vmem = pl.BlockSpec(memory_space=pltpu.VMEM)
    dma = pltpu.SemaphoreType.DMA
    args = (grad_parts, weight, row_state.reshape(1, R), col_state.reshape(GROUPS, 128))
    update, new_row, new_col = pl.pallas_call(
        kernel,
        out_shape=(
            jax.ShapeDtypeStruct((R, OWN), F32),
            jax.ShapeDtypeStruct((1, R), F32),
            jax.ShapeDtypeStruct((GROUPS, 128), F32),
        ),
        in_specs=[pl.BlockSpec(memory_space=pltpu.HBM)] * 4,
        out_specs=(vmem, vmem, vmem),
        scratch_shapes=[
            pltpu.VMEM((R, FF), jnp.bfloat16),
            pltpu.VMEM((R, OWN), jnp.bfloat16),
            pltpu.VMEM((1, R), F32),
            pltpu.VMEM((GROUPS, 128), F32),
            pltpu.VMEM((2, 4, 4, R, HALF), F32),
            pltpu.VMEM((2, 4, 4, R, HALF), F32),
            pltpu.VMEM((2, 4, 4, R, HALF), F32),
            pltpu.VMEM((2, 2, 2, R, HALF), F32),
            pltpu.VMEM((2, 2, 4, R, HALF), F32),
            pltpu.VMEM((2, 4, R, HALF), F32),
            pltpu.VMEM((2, R, HALF), F32),
            pltpu.VMEM((2, 2, R, HALF), F32),
            pltpu.VMEM((R, OWN), F32),
            pltpu.VMEM((Z, 1, 128), F32),
            pltpu.VMEM((PLANE, 1, 128), F32),
            pltpu.VMEM((GROUPS, 2, 128), F32),
            pltpu.VMEM((Z, 2, 128), F32),
            pltpu.VMEM((Z, 2, 128), F32),
            pltpu.VMEM((GROUPS, 2, 128), F32),
            pltpu.VMEM((PLANE, 2, 128), F32),
            dma((4,)),
            dma((8,)), dma((8,)),
            dma((2, 6)), dma((2, 6)),
            dma((2, 6)), dma((2, 6)),
            dma, dma,
            dma, dma,
            dma, dma,
            dma((4,)), dma,
            dma((2,)), dma((GROUPS,)),
            dma, dma,
            pltpu.SemaphoreType.REGULAR, pltpu.SemaphoreType.REGULAR,
        ],
        compiler_params=pltpu.CompilerParams(
            collective_id=0, has_side_effects=True, vmem_limit_bytes=48 * 2**20
        ),
    )(*(pltpu.with_memory_space_constraint(a, pltpu.HBM) for a in args))
    return update, new_row.reshape(R), new_col.reshape(OWN)


def solution(mesh):
    return jax.shard_map(
        on_device,
        mesh=mesh,
        in_specs=(
            P(("dp", "narrow"), "wide", None),
            P("wide", ("dp", "narrow")),
            P("wide"),
            P(("dp", "narrow")),
        ),
        out_specs=(P("wide", ("dp", "narrow")), P("wide"), P(("dp", "narrow"))),
        check_vma=False,
    )
```

time: 90.5 us -> 74.1 us (0.82)
  Pallas kernels: 84.4 us -> 71.5 us
  local copies, waits for them, and re-layouts: 5.14 us -> 1.75 us
    pallas_call x1, Pallas kernels: 84.4 us -> 71.5 us  [on_device(): pl.pallas_call(kernel, out_shape=(jax.ShapeDtypeStruct((R, OWN), F32), ja...]
    unnamed x11 -> x3, local copies, waits for them, and re-layouts: 5.14 us -> 1.75 us
where the time goes in v2:
time: 74.1 us; the launch traced here: 73.9 us
  Pallas kernels  71.5 us (96%)
  local copies, waits for them, and re-layouts  1.75 us (2%)
    pallas_call x1, Pallas kernels, on_device(): pl.pallas_call(kernel, out_shape=(jax.ShapeDtypeStruct((R, OWN), F32), ja...  71.5 us
    unnamed x3, local copies, waits for them, and re-layouts  1.75 us

profile of v2, /device:TPU:1, one launch (start us, length us, event | category | flops | bytes accessed | tf_op | source)
XLA Modules:
  0.0 73.9 jit_solution(7893189890979815713)
XLA Ops:
  0.6 71.5 %shard_map.67 = (f32[8,2304]{1,0:T(8,128)S(1)}, f32[1,8]{1,0:T(1,128)S(1)}, f32[18,128]{1,0:T(8,128)S(1)}) custom-call(bf16[1,8,73728]{2,1,0:T(8,128)(2,1)} %g_hbm.1, bf16[8,2304]{1,0:T(8,128)(2,1)} %w_hbm.1, f32[1,8]{1,0:T(1,128)} %bitcast.7, f32[18,128]{1,0:T(8,128)} %bitcast.6), custom_call_target="tpu_custom_call" | custom-call | tf_op jit(solution)/shard_map/pallas_call | solution.py:362
  72.1 0.6 copy.10
  72.8 0.5 copy.11
  73.3 0.6 copy.12

commit v3 on v0

v3 whole, which is shorter than its diff:
```python
import jax
import jax.numpy as jnp
from jax import lax
from jax.experimental import pallas as pl
from jax.experimental.pallas import tpu as pltpu
from jax.sharding import PartitionSpec as P

FF = 73728
ROWS = 256
STEP = 100
BETA = 1.0 - STEP ** (-0.8)

MESH = pl.DeviceIdType.MESH
F32 = jnp.float32
R = 8
OWN = 2304
HALF = OWN // 2
GROUPS = OWN // 128
PLANE = 32
Z = 32
COPIES = 2
APART = Z // COPIES
EACH = 16 // APART

ORDER = ((0, 2), (1, 2), (0, 1), (1, 1), (0, 3), (1, 3), (0, 0), (1, 0))


def chip(x, y, z, c):
    return (x * 2 + y % 2, z, (y // 2) * 2 + c)


def far_first(i, far):
    return far + ((i + 1) // 2) * (2 * ((i + 1) % 2) - 1)


def kernel(
    g_hbm, w_hbm, row_hbm, col_hbm,
    upd_ref, nrow_ref, ncol_ref,
    gbuf, w_ref, row_ref, col_ref, part, pair, acc, r1, r2, red, s2, grad,
    wz, rz, csrc, tsrc, cz, tz, cz2, tz2, call, tall, fz,
    load_sem, p_send, p_recv, a_send, a_recv, b_send, b_recv,
    one_send, one_recv, x_send, x_recv, ag_send, ag_recv,
    rows_in, reach2, reach4, reach8,
):
    dp = lax.axis_index("dp")
    z = lax.axis_index("wide")
    nr = lax.axis_index("narrow")
    x, y, core = dp // 2, (nr // 2) * 2 + dp % 2, nr % 2
    me = dp * 4 + nr
    other = chip(x, y, z, 1 - core)

    sent = []

    loads = [
        pltpu.make_async_copy(src, dst, load_sem.at[i])
        for i, (src, dst) in enumerate(
            ((g_hbm.at[0], gbuf), (w_hbm, w_ref), (row_hbm, row_ref), (col_hbm, col_ref)))
    ]
    for load in loads:
        load.start()

    def near(axis, s):
        if axis == 0:
            return chip((x + s) % 4, y, z, core)
        return chip(x, (y + s) % 4, z, core)

    def plane_peer(j):
        t = (me + j) % PLANE
        return (t // 4, z, t % 4)

    def z_peer(j):
        return (dp, (z + j) % Z, nr)

    def signal(sem, device):
        pl.semaphore_signal(sem, inc=1, device_id=device, device_id_type=MESH)

    def remote(src, dst, send, recv, device):
        return pltpu.make_async_remote_copy(src, dst, send, recv, device, MESH)

    def bytes_of(ref, send, recv):
        return remote(ref, ref, send, recv, other)

    barrier = pltpu.get_barrier_semaphore()
    signal(barrier, other)
    for s in (1, 3, 2):
        signal(barrier, near(0, s))
        signal(barrier, near(1, s))
        signal(barrier, chip((x + s) % 4, y, z, 1 - core))
    for s in (1, 2):
        signal(barrier, z_peer(s))
        signal(barrier, z_peer(Z - s))

    for load in loads[1:]:
        load.wait()
    wacc = jnp.zeros((R, 128), F32)
    for k in range(GROUPS):
        wk = w_ref[:, k * 128:(k + 1) * 128].astype(F32)
        wacc = wacc + wk * wk
    wz[z] = jnp.sum(wacc, axis=0, keepdims=True)

    def cols(h, d, e, c):
        tx = (x + (d if h == 0 else e)) % 4
        ty = (y + (e if h == 0 else d)) % 4
        owner = ((tx * 2 + ty % 2) * 2 + ty // 2) * 2 + c
        return pl.ds(pl.multiple_of(owner * OWN + h * HALF, 128), HALF)

    loads[0].wait()
    swaps = []
    for i, (h, d) in enumerate(ORDER):
        for e in range(4):
            part[h, d, e] = gbuf[:, cols(h, d, e, 1 - core)].astype(F32)
        if i == 0:
            pl.semaphore_wait(barrier, 14)
        copy = remote(part.at[h, d], pair.at[h, d], p_send.at[i], p_recv.at[i], other)
        copy.start()
        swaps.append(copy)
        sent.append(copy.wait_send)

    for s in (1, 2, 3):
        signal(rows_in, near(1, s))
    signal(reach2, z_peer(2))
    signal(reach2, z_peer(Z - 2))

    relay = [[None] * 4, [None] * 4]
    straight = [[None] * 4, [None] * 4]
    onward = [[None] * 4, [None] * 4]
    for h in range(2):
        up, down = near(h, 1), near(h, 3)
        for e in range(4):
            with_relay, against = (up, down) if e % 2 == 0 else (down, up)
            to, back = (0, 1) if e % 2 == 0 else (1, 0)
            relay[h][e] = remote(
                acc.at[h, 2, e], r1.at[h, e], a_send.at[h, 0, e], a_recv.at[h, 0, e], with_relay)
            onward[h][e] = remote(
                acc.at[h, 1 + 2 * to, e], r2.at[h, to, e],
                a_send.at[h, 1, e], a_recv.at[h, 1, e], with_relay)
            straight[h][e] = remote(
                acc.at[h, 1 + 2 * back, e], r2.at[h, back, e],
                a_send.at[h, 2, e], a_recv.at[h, 2, e], against)
            sent.extend(c[h][e].wait_send for c in (relay, onward, straight))

    for i, (h, d) in enumerate(ORDER):
        swaps[i].wait_recv()
        for e in (2, 1, 0, 3):
            acc[h, d, e] = gbuf[:, cols(h, d, e, core)].astype(F32) + pair[h, d, e]
            if d == 2:
                relay[h][e].start()
            elif (d, e) in ((1, 1), (1, 3), (3, 2), (3, 0)):
                straight[h][e].start()

    pl.semaphore_wait(reach2, 2)
    signal(reach4, z_peer(4))
    signal(reach4, z_peer(Z - 4))

    for e in (2, 1, 3, 0):
        for h in range(2):
            d = 1 if e % 2 == 0 else 3
            relay[h][e].wait_recv()
            acc[h, d, e] = acc[h, d, e] + r1[h, e]
            onward[h][e].start()

    second = [[None] * 4, [None] * 4]
    for h in range(2):
        for e in range(1, 4):
            second[h][e] = remote(
                red.at[h, e], s2.at[h, e], b_send.at[h, e], b_recv.at[h, e], near(1 - h, e))
            sent.append(second[h][e].wait_send)

    pl.semaphore_wait(reach4, 2)
    signal(reach8, z_peer(8))
    signal(reach8, z_peer(Z - 8))

    for e in (2, 1, 3, 0):
        for h in range(2):
            straight[h][e].wait_recv()
            onward[h][e].wait_recv()
            red[h, e] = acc[h, 0, e] + r2[h, 0, e] + r2[h, 1, e]
            if e:
                second[h][e].start()

    rowacc = jnp.zeros((R, 128), F32)
    for h in range(2):
        for e in (1, 3, 2):
            second[h][e].wait_recv()
        for k in range(HALF // 128):
            at = pl.ds(k * 128, 128)
            g = (red[h, 0, :, at] + s2[h, 1, :, at]) + (s2[h, 3, :, at] + s2[h, 2, :, at])
            grad[:, h * HALF + k * 128:h * HALF + (k + 1) * 128] = g
            rowacc = rowacc + (g * g + 1e-30)

    diagonal = (lax.broadcasted_iota(jnp.int32, (R, 128), 0)
                == lax.broadcasted_iota(jnp.int32, (R, 128), 1))
    rowsum = jnp.sum(rowacc, axis=1, keepdims=True)
    rz[me] = jnp.sum(jnp.where(diagonal, rowsum, 0.0), axis=0, keepdims=True)
    pl.semaphore_wait(rows_in, 3)

    def to_plane(ref, i):
        @pl.loop(0, PLANE - 1)
        def _(j):
            remote(ref.at[me], ref.at[me], one_send.at[i], one_recv.at[i],
                   plane_peer(far_first(j, PLANE // 2))).start()

        rest = bytes_of(ref.at[pl.ds(1, PLANE - 1)], one_send.at[i], one_recv.at[i])
        sent.append(rest.wait_send)
        return rest.wait_recv

    rows_here = to_plane(rz, 0)

    def first_group(t):
        return (t % APART) * EACH

    def owns_extra(t):
        return t % (APART // 2) == APART // 4

    def extra(t):
        return 16 + (t % APART) // (3 * APART // 4)

    def to_owners(src, at_owner, at_extra, i):
        @pl.loop(0, Z - 1)
        def _(j):
            off = far_first(j, Z // 2)
            remote(src.at[pl.ds(first_group(z + off), EACH)], at_owner.at[z],
                   one_send.at[i], one_recv.at[i], z_peer(off)).start()

        rest = bytes_of(at_owner.at[pl.ds(1, Z - 1)], one_send.at[i], one_recv.at[i])
        sent.append(rest.wait_send)

        def copy(j):
            t = j * (APART // 2) + APART // 4
            return t != z, remote(
                src.at[extra(t)], at_extra.at[z], x_send.at[i, j], x_recv.at[i], (dp, t, nr))

        @pl.loop(0, 2 * COPIES)
        def _(j):
            needed, c = copy(j)
            pl.when(needed)(c.start)

        def sent_extra():
            @pl.loop(0, 2 * COPIES)
            def _(j):
                needed, c = copy(j)
                pl.when(needed)(c.wait_send)

        sent.append(sent_extra)
        at_owner[z] = src[pl.ds(first_group(z), EACH)]
        return rest.wait_recv

    def to_near(ref, k, n, send, recv):
        @pl.loop(0, APART - 1)
        def _(j):
            half = APART // 2
            off = (1 - j % 2) * (Z - half + j // 2) + (j % 2) * (half - 1 - j // 2)
            remote(ref.at[pl.ds(k, n)], ref.at[pl.ds(k, n)], send, recv, z_peer(off)).start()

    def from_near(ref, i):
        @pl.loop(0, APART)
        def _(r):
            @pl.when(r != z % APART)
            def _():
                bytes_of(ref.at[pl.ds(0, EACH)], ag_send.at[i, 0], ag_recv.at[i, r]).wait_recv()

        for q in range(2):
            @pl.when(jnp.logical_not(owns_extra(z) & (extra(z) == 16 + q)))
            def _():
                bytes_of(ref.at[0], ag_send.at[i, 0], ag_recv.at[i, APART + q]).wait_recv()

    def sent_near(ref, i):
        def wait():
            bytes_of(ref.at[pl.ds(0, EACH * (APART - 1))], ag_send.at[i, 0], one_recv.at[0]).wait_send()

            @pl.when(owns_extra(z))
            def _():
                bytes_of(ref.at[pl.ds(0, APART - 1)], ag_send.at[i, 1], one_recv.at[0]).wait_send()

        sent.append(wait)

    for k in range(GROUPS):
        g = grad[:, k * 128:(k + 1) * 128]
        csrc[k] = jnp.sum(g * g + 1e-30, axis=0, keepdims=True)
    pl.semaphore_wait(reach8, 2)
    c_here = to_owners(csrc, cz, cz2, 1)

    rows_here()
    rowtotal = jnp.sum(rz[...], axis=0)
    new_row = BETA * row_ref[...] + (1.0 - BETA) * (rowtotal[:, :R] / FF)
    nrow_ref[...] = new_row
    eye = (lax.broadcasted_iota(jnp.int32, (R, R), 0)
           == lax.broadcasted_iota(jnp.int32, (R, R), 1))
    rows = jnp.sum(jnp.where(eye, jnp.broadcast_to(new_row, (R, R)), 0.0), axis=1, keepdims=True)
    inv_rows = jnp.broadcast_to(1.0 / rows, (R, 128))

    for k in range(GROUPS):
        g = grad[:, k * 128:(k + 1) * 128]
        tsrc[k] = jnp.sum(g * g * inv_rows, axis=0, keepdims=True)
    t_here = to_owners(tsrc, tz, tz2, 2)

    @pl.loop(0, Z - 1)
    def _(j):
        remote(wz.at[z], wz.at[z], one_send.at[3], one_recv.at[3],
               z_peer(far_first(j, Z // 2))).start()

    w_here = bytes_of(wz.at[pl.ds(1, Z - 1)], one_send.at[3], one_recv.at[3])
    sent.append(w_here.wait_send)

    inv_sqrt_rows = jnp.broadcast_to(lax.rsqrt(rows), (R, 128))
    for k in range(GROUPS):
        at = slice(k * 128, (k + 1) * 128)
        grad[:, at] = grad[:, at] * inv_sqrt_rows
    for wait in sent:
        wait()
    sent.clear()

    def new_cols(ref, k):
        return BETA * col_ref[pl.ds(k, 1), :] + (1.0 - BETA) * (ref / ROWS)

    c_here()
    own = jnp.sum(cz[...], axis=0)
    for s in range(EACH):
        call[first_group(z) + s] = new_cols(own[s], first_group(z) + s)
    to_near(call, first_group(z), EACH, ag_send.at[0, 0], ag_recv.at[0, z % APART])

    @pl.when(owns_extra(z))
    def _():
        cz2[z] = csrc[extra(z)]
        bytes_of(cz2.at[pl.ds(1, Z - 1)], one_send.at[0], x_recv.at[1]).wait_recv()
        call[extra(z)] = new_cols(jnp.sum(cz2[...], axis=0), extra(z))
        to_near(call, extra(z), 1, ag_send.at[0, 1], ag_recv.at[0, APART + extra(z) - 16])

    sent_near(call, 0)

    t_here()
    own = jnp.sum(tz[...], axis=0)
    for s in range(EACH):
        tall[first_group(z) + s] = own[s] / call[first_group(z) + s]
    to_near(tall, first_group(z), EACH, ag_send.at[1, 0], ag_recv.at[1, z % APART])

    @pl.when(owns_extra(z))
    def _():
        tz2[z] = tsrc[extra(z)]
        bytes_of(tz2.at[pl.ds(1, Z - 1)], one_send.at[0], x_recv.at[2]).wait_recv()
        tall[extra(z)] = jnp.sum(tz2[...], axis=0) / call[extra(z)]
        to_near(tall, extra(z), 1, ag_send.at[1, 1], ag_recv.at[1, APART + extra(z) - 16])

    sent_near(tall, 1)

    from_near(call, 0)
    for k in range(GROUPS):
        new_col = call[k]
        ncol_ref[k:k + 1] = new_col
        at = slice(k * 128, (k + 1) * 128)
        grad[:, at] = grad[:, at] * lax.rsqrt(new_col)
    w_here.wait_recv()
    fz[me, 1:2] = jnp.sum(wz[...], axis=0)

    from_near(tall, 1)
    fz[me, 0:1] = jnp.sum(tall[...], axis=0)
    sums_here = to_plane(fz, 4)
    for wait in sent:
        wait()
    sums_here()
    total = jnp.sum(jnp.sum(fz[...], axis=0), axis=1, keepdims=True)
    root = jnp.sqrt(total / (ROWS * FF))
    clip = jnp.maximum(1.0, root[0:1])
    weight_rms = jnp.maximum(0.001, root[1:2])
    upd_ref[...] = grad[...] * (weight_rms / clip)


def on_device(grad_parts, weight, row_state, col_state):
    vmem = pl.BlockSpec(memory_space=pltpu.VMEM)
    dma = pltpu.SemaphoreType.DMA
    args = (grad_parts, weight, row_state.reshape(1, R), col_state.reshape(GROUPS, 128))
    update, new_row, new_col = pl.pallas_call(
        kernel,
        out_shape=(
            jax.ShapeDtypeStruct((R, OWN), F32),
            jax.ShapeDtypeStruct((1, R), F32),
            jax.ShapeDtypeStruct((GROUPS, 128), F32),
        ),
        in_specs=[pl.BlockSpec(memory_space=pltpu.HBM)] * 4,
        out_specs=(vmem, vmem, vmem),
        scratch_shapes=[
            pltpu.VMEM((R, FF), jnp.bfloat16),
            pltpu.VMEM((R, OWN), jnp.bfloat16),
            pltpu.VMEM((1, R), F32),
            pltpu.VMEM((GROUPS, 128), F32),
            pltpu.VMEM((2, 4, 4, R, HALF), F32),
            pltpu.VMEM((2, 4, 4, R, HALF), F32),
            pltpu.VMEM((2, 4, 4, R, HALF), F32),
            pltpu.VMEM((2, 4, R, HALF), F32),
            pltpu.VMEM((2, 2, 4, R, HALF), F32),
            pltpu.VMEM((2, 4, R, HALF), F32),
            pltpu.VMEM((2, 4, R, HALF), F32),
            pltpu.VMEM((R, OWN), F32),
            pltpu.VMEM((Z, 1, 128), F32),
            pltpu.VMEM((PLANE, 1, 128), F32),
            pltpu.VMEM((GROUPS, 1, 128), F32),
            pltpu.VMEM((GROUPS, 1, 128), F32),
            pltpu.VMEM((Z, EACH, 1, 128), F32),
            pltpu.VMEM((Z, EACH, 1, 128), F32),
            pltpu.VMEM((Z, 1, 128), F32),
            pltpu.VMEM((Z, 1, 128), F32),
            pltpu.VMEM((GROUPS, 1, 128), F32),
            pltpu.VMEM((GROUPS, 1, 128), F32),
            pltpu.VMEM((PLANE, 2, 128), F32),
            dma((4,)),
            dma((8,)), dma((8,)),
            dma((2, 3, 4)), dma((2, 3, 4)),
            dma((2, 4)), dma((2, 4)),
            dma((5,)), dma((5,)),
            dma((3, 2 * COPIES)), dma((3,)),
            dma((2, 2)), dma((2, APART + 2)),
            *[pltpu.SemaphoreType.REGULAR] * 4,
        ],
        compiler_params=pltpu.CompilerParams(
            collective_id=0, has_side_effects=True, vmem_limit_bytes=48 * 2**20
        ),
    )(*(pltpu.with_memory_space_constraint(a, pltpu.HBM) for a in args))
    return update, new_row.reshape(R), new_col.reshape(OWN)


def solution(mesh):
    return jax.shard_map(
        on_device,
        mesh=mesh,
        in_specs=(
            P(("dp", "narrow"), "wide", None),
            P("wide", ("dp", "narrow")),
            P("wide"),
            P(("dp", "narrow")),
        ),
        out_specs=(P("wide", ("dp", "narrow")), P("wide"), P(("dp", "narrow"))),
        check_vma=False,
    )
```

time: 510 us -> 67.7 us (0.13)
  blocking collectives: 327 us -> 0 us
  waiting for transfers between devices: 160 us -> 0 us
  Pallas kernels: 0 us -> 65.1 us
  between operations: 15.4 us -> 0.64 us
  other arithmetic: 7.67 us -> 0 us
    psum x3 -> x0, blocking collectives: 327 us -> none  [the longest x1 152 us: on_device(): update_sum = lax.psum(jnp.sum(scaled * scaled), ('dp', 'wide', 'narrow'))]
    reduce_scatter x1 -> x0, waiting for transfers between devices: 160 us -> none  [on_device(): lax.psum_scatter(local_part, ('dp', 'narrow'), scatter_dimension=1, tiled...]
    pallas_call x0 -> x1, Pallas kernels: none -> 65.1 us  [on_device(): pl.pallas_call(kernel, out_shape=(jax.ShapeDtypeStruct((R, OWN), F32), ja...]
  transfers between devices with their start and end apart: 1 -> 0, of which waited for: 1 -> 0; matrix products, arithmetic and copies ran while one was open for 0% -> 0% of each run, Pallas kernels for 0% -> 0%
where the time goes in v3:
time: 67.7 us; the launch traced here: 67.5 us
  Pallas kernels  65.1 us (96%)
  local copies, waits for them, and re-layouts  1.75 us (3%)
    pallas_call x1, Pallas kernels, on_device(): pl.pallas_call(kernel, out_shape=(jax.ShapeDtypeStruct((R, OWN), F32), ja...  65.1 us
    unnamed x3, local copies, waits for them, and re-layouts  1.75 us

profile of v3, /device:TPU:1, one launch (start us, length us, event | category | flops | bytes accessed | tf_op | source)
XLA Modules:
  0.0 67.5 jit_solution(8586954016543966569)
XLA Ops:
  0.6 65.1 %shard_map.67 = (f32[8,2304]{1,0:T(8,128)S(1)}, f32[1,8]{1,0:T(1,128)S(1)}, f32[18,128]{1,0:T(8,128)S(1)}) custom-call(bf16[1,8,73728]{2,1,0:T(8,128)(2,1)} %g_hbm.1, bf16[8,2304]{1,0:T(8,128)(2,1)} %w_hbm.1, f32[1,8]{1,0:T(1,128)} %bitcast.7, f32[18,128]{1,0:T(8,128)} %bitcast.6), custom_call_target="tpu_custom_call" | custom-call | tf_op jit(solution)/shard_map/pallas_call | solution.py:372
  65.8 0.6 copy.10
  66.4 0.5 copy.11
  66.9 0.6 copy.12

commit v4 on v3

v4 whole, which is shorter than its diff:
```python
import jax
import jax.numpy as jnp
from jax import lax
from jax.experimental import pallas as pl
from jax.experimental.pallas import tpu as pltpu
from jax.sharding import PartitionSpec as P

FF = 73728
ROWS = 256
STEP = 100
BETA = 1.0 - STEP ** (-0.8)

MESH = pl.DeviceIdType.MESH
F32 = jnp.float32
R = 8
OWN = 2304
HALF = OWN // 2
GROUPS = OWN // 128
PLANE = 32
Z = 32
PAD = 24

ORDER = ((0, 2), (1, 2), (0, 1), (1, 1), (0, 3), (1, 3), (0, 0), (1, 0))


def chip(x, y, z, c):
    return (x * 2 + y % 2, z, (y // 2) * 2 + c)


def far_first(i, far):
    return far + ((i + 1) // 2) * (2 * ((i + 1) % 2) - 1)


def kernel(
    g_hbm, w_hbm, row_hbm, col_hbm,
    upd_ref, nrow_ref, ncol_ref,
    gbuf, w_ref, row_ref, col_ref, part, pair, acc, r1, r2, red, s2, grad,
    rz, csrc, tsrc, cz, tz, call, fz, final,
    load_sem, p_send, p_recv, a_send, a_recv, b_send, b_recv,
    one_send, one_recv, rows_in,
):
    dp = lax.axis_index("dp")
    z = lax.axis_index("wide")
    nr = lax.axis_index("narrow")
    x, y, core = dp // 2, (nr // 2) * 2 + dp % 2, nr % 2
    me = dp * 4 + nr
    other = chip(x, y, z, 1 - core)

    sent = []

    loads = [
        pltpu.make_async_copy(src, dst, load_sem.at[i])
        for i, (src, dst) in enumerate(
            ((g_hbm.at[0], gbuf), (w_hbm, w_ref), (row_hbm, row_ref), (col_hbm, col_ref)))
    ]
    for load in loads:
        load.start()

    def near(axis, s):
        if axis == 0:
            return chip((x + s) % 4, y, z, core)
        return chip(x, (y + s) % 4, z, core)

    def plane_peer(j):
        t = (me + j) % PLANE
        return (t // 4, z, t % 4)

    def signal(sem, device):
        pl.semaphore_signal(sem, inc=1, device_id=device, device_id_type=MESH)

    def remote(src, dst, send, recv, device):
        return pltpu.make_async_remote_copy(src, dst, send, recv, device, MESH)

    def bytes_of(ref, send, recv):
        return remote(ref, ref, send, recv, other)

    barrier = pltpu.get_barrier_semaphore()
    signal(barrier, other)
    for s in (1, 3, 2):
        signal(barrier, near(0, s))
        signal(barrier, near(1, s))
        signal(barrier, chip((x + s) % 4, y, z, 1 - core))

    @pl.when(z == 0)
    def _():
        @pl.loop(1, Z)
        def _(j):
            signal(barrier, (dp, j, nr))

    for load in loads[1:]:
        load.wait()
    wacc = jnp.zeros((R, 128), F32)
    for k in range(GROUPS):
        wk = w_ref[:, k * 128:(k + 1) * 128].astype(F32)
        wacc = wacc + wk * wk
    wsum = jnp.sum(wacc, axis=0, keepdims=True)

    def cols(h, d, e, c):
        tx = (x + (d if h == 0 else e)) % 4
        ty = (y + (e if h == 0 else d)) % 4
        owner = ((tx * 2 + ty % 2) * 2 + ty // 2) * 2 + c
        return pl.ds(pl.multiple_of(owner * OWN + h * HALF, 128), HALF)

    loads[0].wait()
    swaps = []
    for i, (h, d) in enumerate(ORDER):
        for e in range(4):
            part[h, d, e] = gbuf[:, cols(h, d, e, 1 - core)].astype(F32)
        if i == 0:
            pl.when(z == 0)(lambda: pl.semaphore_wait(barrier, 10))
            pl.when(z != 0)(lambda: pl.semaphore_wait(barrier, 11))
        copy = remote(part.at[h, d], pair.at[h, d], p_send.at[i], p_recv.at[i], other)
        copy.start()
        swaps.append(copy)
        sent.append(copy.wait_send)

    for s in (1, 2, 3):
        signal(rows_in, near(1, s))

    relay = [[None] * 4, [None] * 4]
    straight = [[None] * 4, [None] * 4]
    onward = [[None] * 4, [None] * 4]
    for h in range(2):
        up, down = near(h, 1), near(h, 3)
        for e in range(4):
            with_relay, against = (up, down) if e % 2 == 0 else (down, up)
            to, back = (0, 1) if e % 2 == 0 else (1, 0)
            relay[h][e] = remote(
                acc.at[h, 2, e], r1.at[h, e], a_send.at[h, 0, e], a_recv.at[h, 0, e], with_relay)
            onward[h][e] = remote(
                acc.at[h, 1 + 2 * to, e], r2.at[h, to, e],
                a_send.at[h, 1, e], a_recv.at[h, 1, e], with_relay)
            straight[h][e] = remote(
                acc.at[h, 1 + 2 * back, e], r2.at[h, back, e],
                a_send.at[h, 2, e], a_recv.at[h, 2, e], against)
            sent.extend(c[h][e].wait_send for c in (relay, onward, straight))

    for i, (h, d) in enumerate(ORDER):
        swaps[i].wait_recv()
        for e in (2, 1, 0, 3):
            acc[h, d, e] = gbuf[:, cols(h, d, e, core)].astype(F32) + pair[h, d, e]
            if d == 2:
                relay[h][e].start()
            elif (d, e) in ((1, 1), (1, 3), (3, 2), (3, 0)):
                straight[h][e].start()

    for e in (2, 1, 3, 0):
        for h in range(2):
            d = 1 if e % 2 == 0 else 3
            relay[h][e].wait_recv()
            acc[h, d, e] = acc[h, d, e] + r1[h, e]
            onward[h][e].start()

    second = [[None] * 4, [None] * 4]
    for h in range(2):
        for e in range(1, 4):
            second[h][e] = remote(
                red.at[h, e], s2.at[h, e], b_send.at[h, e], b_recv.at[h, e], near(1 - h, e))
            sent.append(second[h][e].wait_send)

    for e in (2, 1, 3, 0):
        for h in range(2):
            straight[h][e].wait_recv()
            onward[h][e].wait_recv()
            red[h, e] = acc[h, 0, e] + r2[h, 0, e] + r2[h, 1, e]
            if e:
                second[h][e].start()

    rowacc = jnp.zeros((R, 128), F32)
    for h in range(2):
        for e in (1, 3, 2):
            second[h][e].wait_recv()
        for k in range(HALF // 128):
            at = pl.ds(k * 128, 128)
            g = (red[h, 0, :, at] + s2[h, 1, :, at]) + (s2[h, 3, :, at] + s2[h, 2, :, at])
            grad[:, h * HALF + k * 128:h * HALF + (k + 1) * 128] = g
            rowacc = rowacc + (g * g + 1e-30)

    diagonal = (lax.broadcasted_iota(jnp.int32, (R, 128), 0)
                == lax.broadcasted_iota(jnp.int32, (R, 128), 1))
    rowsum = jnp.sum(rowacc, axis=1, keepdims=True)
    tsrc[GROUPS:] = jnp.zeros((PAD - GROUPS, 128), F32)
    rz[me] = jnp.sum(jnp.where(diagonal, rowsum, 0.0), axis=0, keepdims=True)
    pl.semaphore_wait(rows_in, 3)

    def to_plane(ref, i):
        @pl.loop(0, PLANE - 1)
        def _(j):
            remote(ref.at[me], ref.at[me], one_send.at[i], one_recv.at[i],
                   plane_peer(far_first(j, PLANE // 2))).start()

        rest = bytes_of(ref.at[pl.ds(1, PLANE - 1)], one_send.at[i], one_recv.at[i])
        sent.append(rest.wait_send)
        return rest.wait_recv

    rows_here = to_plane(rz, 0)

    base = z == 0
    to_base = (dp, 0, nr)

    def send_all(src, dst, i):
        @pl.loop(1, Z)
        def _(j):
            t = (j % 2) * ((j + 1) // 2) + (1 - j % 2) * (Z - j // 2)
            remote(src, dst, one_send.at[i], one_recv.at[i], (dp, t, nr)).start()

    csrc[GROUPS:] = jnp.broadcast_to(wsum, (PAD - GROUPS, 128))
    for k in range(GROUPS):
        g = grad[:, k * 128:(k + 1) * 128]
        csrc[k:k + 1] = jnp.sum(g * g + 1e-30, axis=0, keepdims=True)
    c_copy = remote(csrc, cz.at[z], one_send.at[1], one_recv.at[1], to_base)
    t_copy = remote(tsrc, tz.at[z], one_send.at[2], one_recv.at[2], to_base)

    @pl.when(jnp.logical_not(base))
    def _():
        c_copy.start()

    rows_here()
    rowtotal = jnp.sum(rz[...], axis=0)
    new_row = BETA * row_ref[...] + (1.0 - BETA) * (rowtotal[:, :R] / FF)
    eye = (lax.broadcasted_iota(jnp.int32, (R, R), 0)
           == lax.broadcasted_iota(jnp.int32, (R, R), 1))
    rows = jnp.sum(jnp.where(eye, jnp.broadcast_to(new_row, (R, R)), 0.0), axis=1, keepdims=True)
    inv_rows = jnp.broadcast_to(1.0 / rows, (R, 128))

    for k in range(GROUPS):
        g = grad[:, k * 128:(k + 1) * 128]
        tsrc[k:k + 1] = jnp.sum(g * g * inv_rows, axis=0, keepdims=True)

    @pl.when(jnp.logical_not(base))
    def _():
        t_copy.start()

    nrow_ref[...] = new_row
    inv_sqrt_rows = jnp.broadcast_to(lax.rsqrt(rows), (R, 128))
    for k in range(GROUPS):
        at = slice(k * 128, (k + 1) * 128)
        grad[:, at] = grad[:, at] * inv_sqrt_rows
    for wait in sent:
        wait()
    sent.clear()

    @pl.when(base)
    def _():
        cz[0] = csrc[...]
        bytes_of(cz.at[pl.ds(1, Z - 1)], one_send.at[1], one_recv.at[1]).wait_recv()
        sums = jnp.sum(cz[...], axis=0)
        col = BETA * col_ref[...] + (1.0 - BETA) * (sums[:GROUPS] / ROWS)
        call[0:GROUPS] = col
        call[GROUPS:] = jnp.zeros((PAD - GROUPS, 128), F32)
        send_all(call, call, 5)
        fz[me, 1:2] = sums[GROUPS:GROUPS + 1]
        tz[0] = tsrc[...]
        bytes_of(tz.at[pl.ds(1, Z - 1)], one_send.at[1], one_recv.at[2]).wait_recv()
        total = jnp.sum(tz[...], axis=0)[:GROUPS] / col
        fz[me, 0:1] = jnp.sum(total, axis=0, keepdims=True)
        sums_here = to_plane(fz, 4)
        del sent[:]
        sums_here()
        final[...] = jnp.sum(fz[...], axis=0)
        send_all(final, final, 6)

    @pl.when(jnp.logical_not(base))
    def _():
        c_copy.wait_send()
        t_copy.wait_send()
        bytes_of(call, one_send.at[1], one_recv.at[5]).wait_recv()

    for k in range(GROUPS):
        new_col = call[k:k + 1]
        at = slice(k * 128, (k + 1) * 128)
        grad[:, at] = grad[:, at] * lax.rsqrt(new_col)
    ncol_ref[...] = call[0:GROUPS]

    @pl.when(jnp.logical_not(base))
    def _():
        bytes_of(final, one_send.at[1], one_recv.at[6]).wait_recv()

    root = jnp.sqrt(jnp.sum(final[...], axis=1, keepdims=True) / (ROWS * FF))
    clip = jnp.maximum(1.0, root[0:1])
    weight_rms = jnp.maximum(0.001, root[1:2])
    upd_ref[...] = grad[...] * (weight_rms / clip)

    @pl.when(base)
    def _():
        bytes_of(cz.at[pl.ds(1, Z - 1)], one_send.at[5], one_recv.at[5]).wait_send()
        bytes_of(fz.at[pl.ds(1, PLANE - 1)], one_send.at[4], one_recv.at[4]).wait_send()
        bytes_of(fz.at[pl.ds(1, Z - 1)], one_send.at[6], one_recv.at[6]).wait_send()


def on_device(grad_parts, weight, row_state, col_state):
    vmem = pl.BlockSpec(memory_space=pltpu.VMEM)
    dma = pltpu.SemaphoreType.DMA
    args = (grad_parts, weight, row_state.reshape(1, R), col_state.reshape(GROUPS, 128))
    update, new_row, new_col = pl.pallas_call(
        kernel,
        out_shape=(
            jax.ShapeDtypeStruct((R, OWN), F32),
            jax.ShapeDtypeStruct((1, R), F32),
            jax.ShapeDtypeStruct((GROUPS, 128), F32),
        ),
        in_specs=[pl.BlockSpec(memory_space=pltpu.HBM)] * 4,
        out_specs=(vmem, vmem, vmem),
        scratch_shapes=[
            pltpu.VMEM((R, FF), jnp.bfloat16),
            pltpu.VMEM((R, OWN), jnp.bfloat16),
            pltpu.VMEM((1, R), F32),
            pltpu.VMEM((GROUPS, 128), F32),
            pltpu.VMEM((2, 4, 4, R, HALF), F32),
            pltpu.VMEM((2, 4, 4, R, HALF), F32),
            pltpu.VMEM((2, 4, 4, R, HALF), F32),
            pltpu.VMEM((2, 4, R, HALF), F32),
            pltpu.VMEM((2, 2, 4, R, HALF), F32),
            pltpu.VMEM((2, 4, R, HALF), F32),
            pltpu.VMEM((2, 4, R, HALF), F32),
            pltpu.VMEM((R, OWN), F32),
            pltpu.VMEM((PLANE, 1, 128), F32),
            pltpu.VMEM((PAD, 128), F32),
            pltpu.VMEM((PAD, 128), F32),
            pltpu.VMEM((Z, PAD, 128), F32),
            pltpu.VMEM((Z, PAD, 128), F32),
            pltpu.VMEM((PAD, 128), F32),
            pltpu.VMEM((PLANE, 2, 128), F32),
            pltpu.VMEM((2, 128), F32),
            dma((4,)),
            dma((8,)), dma((8,)),
            dma((2, 3, 4)), dma((2, 3, 4)),
            dma((2, 4)), dma((2, 4)),
            dma((7,)), dma((7,)),
            pltpu.SemaphoreType.REGULAR,
        ],
        compiler_params=pltpu.CompilerParams(
            collective_id=0, has_side_effects=True, vmem_limit_bytes=48 * 2**20
        ),
    )(*(pltpu.with_memory_space_constraint(a, pltpu.HBM) for a in args))
    return update, new_row.reshape(R), new_col.reshape(OWN)


def solution(mesh):
    return jax.shard_map(
        on_device,
        mesh=mesh,
        in_specs=(
            P(("dp", "narrow"), "wide", None),
            P("wide", ("dp", "narrow")),
            P("wide"),
            P(("dp", "narrow")),
        ),
        out_specs=(P("wide", ("dp", "narrow")), P("wide"), P(("dp", "narrow"))),
        check_vma=False,
    )
```

time: 67.7 us -> 63.1 us (0.932)
  Pallas kernels: 65.1 us -> 60.5 us
    pallas_call x1, Pallas kernels: 65.1 us -> 60.5 us  [on_device(): pl.pallas_call(kernel, out_shape=(jax.ShapeDtypeStruct((R, OWN), F32), ja...]
where the time goes in v4:
time: 63.1 us; the launch traced here: 62.9 us
  Pallas kernels  60.5 us (96%)
  local copies, waits for them, and re-layouts  1.75 us (3%)
  between operations  0.64 us (1%)
    pallas_call x1, Pallas kernels, on_device(): pl.pallas_call(kernel, out_shape=(jax.ShapeDtypeStruct((R, OWN), F32), ja...  60.5 us
    unnamed x3, local copies, waits for them, and re-layouts  1.75 us

profile of v4, /device:TPU:1, one launch (start us, length us, event | category | flops | bytes accessed | tf_op | source)
XLA Modules:
  0.0 62.9 jit_solution(9098084171226283347)
XLA Ops:
  0.6 60.5 %shard_map.67 = (f32[8,2304]{1,0:T(8,128)S(1)}, f32[1,8]{1,0:T(1,128)S(1)}, f32[18,128]{1,0:T(8,128)S(1)}) custom-call(bf16[1,8,73728]{2,1,0:T(8,128)(2,1)} %g_hbm.1, bf16[8,2304]{1,0:T(8,128)(2,1)} %w_hbm.1, f32[1,8]{1,0:T(1,128)} %bitcast.7, f32[18,128]{1,0:T(8,128)} %bitcast.6), custom_call_target="tpu_custom_call" | custom-call | tf_op jit(solution)/shard_map/pallas_call | solution.py:295
  61.2 0.6 %copy.10 = f32[8,2304]{1,0:T(8,128)} copy(f32[8,2304]{1,0:T(8,128)S(1)} %get-tuple-element.12) | data formatting | bytes 147456
  61.8 0.5 copy.11
  62.3 0.6 copy.12

commit v5 on v4

--- a/solution.py
+++ b/solution.py
@@ -18,6 +18,7 @@
 GROUPS = OWN // 128
 PLANE = 32
 Z = 32
+SOON = 4
 PAD = 24
 
 ORDER = ((0, 2), (1, 2), (0, 1), (1, 1), (0, 3), (1, 3), (0, 0), (1, 0))
@@ -37,7 +38,7 @@
     gbuf, w_ref, row_ref, col_ref, part, pair, acc, r1, r2, red, s2, grad,
     rz, csrc, tsrc, cz, tz, call, fz, final,
     load_sem, p_send, p_recv, a_send, a_recv, b_send, b_recv,
-    one_send, one_recv, rows_in,
+    one_send, one_recv, plane_in,
 ):
     dp = lax.axis_index("dp")
     z = lax.axis_index("wide")
@@ -48,10 +49,15 @@
 
     sent = []
 
+    def slab(i):
+        at = pl.ds(pl.multiple_of(((x + (2, 1, 3, 0)[i]) % 4) * (FF // 4), 128), FF // 4)
+        return g_hbm.at[0, :, at], gbuf.at[:, at]
+
     loads = [
         pltpu.make_async_copy(src, dst, load_sem.at[i])
         for i, (src, dst) in enumerate(
-            ((g_hbm.at[0], gbuf), (w_hbm, w_ref), (row_hbm, row_ref), (col_hbm, col_ref)))
+            (slab(0), slab(1), slab(2), slab(3),
+             (w_hbm, w_ref), (row_hbm, row_ref), (col_hbm, col_ref)))
     ]
     for load in loads:
         load.start()
@@ -74,26 +80,16 @@
     def bytes_of(ref, send, recv):
         return remote(ref, ref, send, recv, other)
 
+    beside = (other, near(0, 1), near(0, 3), near(1, 1), near(1, 3))
     barrier = pltpu.get_barrier_semaphore()
-    signal(barrier, other)
-    for s in (1, 3, 2):
-        signal(barrier, near(0, s))
-        signal(barrier, near(1, s))
-        signal(barrier, chip((x + s) % 4, y, z, 1 - core))
+    for device in beside:
+        signal(barrier, device)
 
     @pl.when(z == 0)
     def _():
         @pl.loop(1, Z)
         def _(j):
             signal(barrier, (dp, j, nr))
-
-    for load in loads[1:]:
-        load.wait()
-    wacc = jnp.zeros((R, 128), F32)
-    for k in range(GROUPS):
-        wk = w_ref[:, k * 128:(k + 1) * 128].astype(F32)
-        wacc = wacc + wk * wk
-    wsum = jnp.sum(wacc, axis=0, keepdims=True)
 
     def cols(h, d, e, c):
         tx = (x + (d if h == 0 else e)) % 4
@@ -101,21 +97,28 @@
         owner = ((tx * 2 + ty % 2) * 2 + ty // 2) * 2 + c
         return pl.ds(pl.multiple_of(owner * OWN + h * HALF, 128), HALF)
 
-    loads[0].wait()
     swaps = []
     for i, (h, d) in enumerate(ORDER):
+        for load in loads[:1] if i == 0 else loads[1:4] if i == 1 else ():
+            load.wait()
         for e in range(4):
             part[h, d, e] = gbuf[:, cols(h, d, e, 1 - core)].astype(F32)
         if i == 0:
-            pl.when(z == 0)(lambda: pl.semaphore_wait(barrier, 10))
-            pl.when(z != 0)(lambda: pl.semaphore_wait(barrier, 11))
+            pl.when(z == 0)(lambda: pl.semaphore_wait(barrier, 5))
+            pl.when(z != 0)(lambda: pl.semaphore_wait(barrier, 6))
         copy = remote(part.at[h, d], pair.at[h, d], p_send.at[i], p_recv.at[i], other)
         copy.start()
         swaps.append(copy)
         sent.append(copy.wait_send)
 
-    for s in (1, 2, 3):
-        signal(rows_in, near(1, s))
+    def tell(r):
+        if r > 0:
+            pl.semaphore_wait(plane_in.at[r - 1], 5)
+        if r < 4:
+            for device in beside:
+                signal(plane_in.at[r], device)
+
+    tell(0)
 
     relay = [[None] * 4, [None] * 4]
     straight = [[None] * 4, [None] * 4]
@@ -141,8 +144,20 @@
             acc[h, d, e] = gbuf[:, cols(h, d, e, core)].astype(F32) + pair[h, d, e]
             if d == 2:
                 relay[h][e].start()
-            elif (d, e) in ((1, 1), (1, 3), (3, 2), (3, 0)):
-                straight[h][e].start()
+
+    for e in (1, 2, 3, 0):
+        for h in range(2):
+            straight[h][e].start()
+
+    tell(1)
+
+    for load in loads[4:]:
+        load.wait()
+    wacc = jnp.zeros((R, 128), F32)
+    for k in range(GROUPS):
+        wk = w_ref[:, k * 128:(k + 1) * 128].astype(F32)
+        wacc = wacc + wk * wk
+    wsum = jnp.sum(wacc, axis=0, keepdims=True)
 
     for e in (2, 1, 3, 0):
         for h in range(2):
@@ -150,6 +165,8 @@
             relay[h][e].wait_recv()
             acc[h, d, e] = acc[h, d, e] + r1[h, e]
             onward[h][e].start()
+
+    tell(2)
 
     second = [[None] * 4, [None] * 4]
     for h in range(2):
@@ -166,6 +183,7 @@
             if e:
                 second[h][e].start()
 
+    tell(3)
     rowacc = jnp.zeros((R, 128), F32)
     for h in range(2):
         for e in (1, 3, 2):
@@ -181,7 +199,7 @@
     rowsum = jnp.sum(rowacc, axis=1, keepdims=True)
     tsrc[GROUPS:] = jnp.zeros((PAD - GROUPS, 128), F32)
     rz[me] = jnp.sum(jnp.where(diagonal, rowsum, 0.0), axis=0, keepdims=True)
-    pl.semaphore_wait(rows_in, 3)
+    tell(4)
 
     def to_plane(ref, i):
         @pl.loop(0, PLANE - 1)
@@ -198,11 +216,10 @@
     base = z == 0
     to_base = (dp, 0, nr)
 
-    def send_all(src, dst, i):
-        @pl.loop(1, Z)
+    def send_along(ref, i, first, last):
+        @pl.loop(first, last)
         def _(j):
-            t = (j % 2) * ((j + 1) // 2) + (1 - j % 2) * (Z - j // 2)
-            remote(src, dst, one_send.at[i], one_recv.at[i], (dp, t, nr)).start()
+            remote(ref, ref, one_send.at[i], one_recv.at[i], (dp, j, nr)).start()
 
     csrc[GROUPS:] = jnp.broadcast_to(wsum, (PAD - GROUPS, 128))
     for k in range(GROUPS):
@@ -248,17 +265,27 @@
         col = BETA * col_ref[...] + (1.0 - BETA) * (sums[:GROUPS] / ROWS)
         call[0:GROUPS] = col
         call[GROUPS:] = jnp.zeros((PAD - GROUPS, 128), F32)
-        send_all(call, call, 5)
+        send_along(call, 5, 1, Z)
+        inv_col = 1.0 / col
         fz[me, 1:2] = sums[GROUPS:GROUPS + 1]
         tz[0] = tsrc[...]
         bytes_of(tz.at[pl.ds(1, Z - 1)], one_send.at[1], one_recv.at[2]).wait_recv()
-        total = jnp.sum(tz[...], axis=0)[:GROUPS] / col
+        total = jnp.sum(tz[...], axis=0)[:GROUPS] * inv_col
         fz[me, 0:1] = jnp.sum(total, axis=0, keepdims=True)
         sums_here = to_plane(fz, 4)
-        del sent[:]
+        sent.clear()
+
+        @pl.loop(0, PLANE)
+        def _(j):
+            for t in range(1, SOON):
+                remote(fz.at[me], fz.at[me], one_send.at[7], one_recv.at[4],
+                       (j // 4, t, j % 4)).start()
+
+        bytes_of(cz.at[pl.ds(1, Z - 1)], one_send.at[5], one_recv.at[5]).wait_send()
+        bytes_of(fz.at[pl.ds(1, PLANE - 1)], one_send.at[4], one_recv.at[4]).wait_send()
+        bytes_of(tz.at[pl.ds(0, 2 * PLANE * (SOON - 1) // PAD)], one_send.at[7], one_recv.at[4]).wait_send()
         sums_here()
         final[...] = jnp.sum(fz[...], axis=0)
-        send_all(final, final, 6)
 
     @pl.when(jnp.logical_not(base))
     def _():
@@ -272,20 +299,27 @@
         grad[:, at] = grad[:, at] * lax.rsqrt(new_col)
     ncol_ref[...] = call[0:GROUPS]
 
-    @pl.when(jnp.logical_not(base))
+    @pl.when(z >= SOON)
     def _():
         bytes_of(final, one_send.at[1], one_recv.at[6]).wait_recv()
+
+    @pl.when((z > 0) & (z < SOON))
+    def _():
+        bytes_of(fz, one_send.at[1], one_recv.at[4]).wait_recv()
+        final[...] = jnp.sum(fz[...], axis=0)
+
+    @pl.when(z == SOON - 1)
+    def _():
+        send_along(final, 6, SOON, Z)
 
     root = jnp.sqrt(jnp.sum(final[...], axis=1, keepdims=True) / (ROWS * FF))
     clip = jnp.maximum(1.0, root[0:1])
     weight_rms = jnp.maximum(0.001, root[1:2])
     upd_ref[...] = grad[...] * (weight_rms / clip)
 
-    @pl.when(base)
-    def _():
-        bytes_of(cz.at[pl.ds(1, Z - 1)], one_send.at[5], one_recv.at[5]).wait_send()
-        bytes_of(fz.at[pl.ds(1, PLANE - 1)], one_send.at[4], one_recv.at[4]).wait_send()
-        bytes_of(fz.at[pl.ds(1, Z - 1)], one_send.at[6], one_recv.at[6]).wait_send()
+    @pl.when(z == SOON - 1)
+    def _():
+        bytes_of(fz.at[pl.ds(0, Z - SOON)], one_send.at[6], one_recv.at[6]).wait_send()
 
 
 def on_device(grad_parts, weight, row_state, col_state):
@@ -322,12 +356,12 @@
             pltpu.VMEM((PAD, 128), F32),
             pltpu.VMEM((PLANE, 2, 128), F32),
             pltpu.VMEM((2, 128), F32),
-            dma((4,)),
+            dma((7,)),
             dma((8,)), dma((8,)),
             dma((2, 3, 4)), dma((2, 3, 4)),
             dma((2, 4)), dma((2, 4)),
-            dma((7,)), dma((7,)),
-            pltpu.SemaphoreType.REGULAR,
+            dma((8,)), dma((8,)),
+            pltpu.SemaphoreType.REGULAR((4,)),
         ],
         compiler_params=pltpu.CompilerParams(
             collective_id=0, has_side_effects=True, vmem_limit_bytes=48 * 2**20

time: 63.1 us -> 61.9 us (0.981)
  Pallas kernels: 60.5 us -> 59.3 us
    pallas_call x1, Pallas kernels: 60.5 us -> 59.3 us  [on_device(): pl.pallas_call(kernel, out_shape=(jax.ShapeDtypeStruct((R, OWN), F32), ja...]
where the time goes in v5:
time: 61.9 us; the launch traced here: 61.7 us
  Pallas kernels  59.3 us (96%)
  local copies, waits for them, and re-layouts  1.75 us (3%)
  between operations  0.64 us (1%)
    pallas_call x1, Pallas kernels, on_device(): pl.pallas_call(kernel, out_shape=(jax.ShapeDtypeStruct((R, OWN), F32), ja...  59.3 us
    unnamed x3, local copies, waits for them, and re-layouts  1.75 us

profile of v5, /device:TPU:1, one launch (start us, length us, event | category | flops | bytes accessed | tf_op | source)
XLA Modules:
  0.0 61.7 jit_solution(1553011174919829954)
XLA Ops:
  0.6 59.3 %shard_map.67 = (f32[8,2304]{1,0:T(8,128)S(1)}, f32[1,8]{1,0:T(1,128)S(1)}, f32[18,128]{1,0:T(8,128)S(1)}) custom-call(bf16[1,8,73728]{2,1,0:T(8,128)(2,1)} %g_hbm.1, bf16[8,2304]{1,0:T(8,128)(2,1)} %w_hbm.1, f32[1,8]{1,0:T(1,128)} %bitcast.7, f32[18,128]{1,0:T(8,128)} %bitcast.6), custom_call_target="tpu_custom_call" | custom-call | tf_op jit(solution)/shard_map/pallas_call | solution.py:329
  60.0 0.6 %copy.10 = f32[8,2304]{1,0:T(8,128)} copy(f32[8,2304]{1,0:T(8,128)S(1)} %get-tuple-element.12) | data formatting | bytes 147456
  60.6 0.5 copy.11
  61.1 0.6 copy.12

commit v6 on v5

--- a/solution.py
+++ b/solution.py
@@ -59,8 +59,6 @@
             (slab(0), slab(1), slab(2), slab(3),
              (w_hbm, w_ref), (row_hbm, row_ref), (col_hbm, col_ref)))
     ]
-    for load in loads:
-        load.start()
 
     def near(axis, s):
         if axis == 0:
@@ -84,6 +82,9 @@
     barrier = pltpu.get_barrier_semaphore()
     for device in beside:
         signal(barrier, device)
+
+    for load in loads:
+        load.start()
 
     @pl.when(z == 0)
     def _():
@@ -240,13 +241,13 @@
     rows = jnp.sum(jnp.where(eye, jnp.broadcast_to(new_row, (R, R)), 0.0), axis=1, keepdims=True)
     inv_rows = jnp.broadcast_to(1.0 / rows, (R, 128))
 
-    for k in range(GROUPS):
-        g = grad[:, k * 128:(k + 1) * 128]
-        tsrc[k:k + 1] = jnp.sum(g * g * inv_rows, axis=0, keepdims=True)
-
-    @pl.when(jnp.logical_not(base))
-    def _():
-        t_copy.start()
+    for first_group in range(0, PAD, 8):
+        for k in range(first_group, min(first_group + 8, GROUPS)):
+            g = grad[:, k * 128:(k + 1) * 128]
+            tsrc[k:k + 1] = jnp.sum(g * g * inv_rows, axis=0, keepdims=True)
+        tile = pl.ds(first_group, 8)
+        piece = remote(tsrc.at[tile], tz.at[z, tile], one_send.at[2], one_recv.at[2], to_base)
+        pl.when(jnp.logical_not(base))(piece.start)
 
     nrow_ref[...] = new_row
     inv_sqrt_rows = jnp.broadcast_to(lax.rsqrt(rows), (R, 128))

time: 61.9 us -> 61.9 us (level)
  no operation moved by 1% of the time
where the time goes in v6:
time: 61.9 us; the launch traced here: 61.7 us
  Pallas kernels  59.3 us (96%)
  local copies, waits for them, and re-layouts  1.75 us (3%)
  between operations  0.64 us (1%)
    pallas_call x1, Pallas kernels, on_device(): pl.pallas_call(kernel, out_shape=(jax.ShapeDtypeStruct((R, OWN), F32), ja...  59.3 us
    unnamed x3, local copies, waits for them, and re-layouts  1.75 us

profile of v6, /device:TPU:1, one launch (start us, length us, event | category | flops | bytes accessed | tf_op | source)
XLA Modules:
  0.0 61.7 jit_solution(12149553329692892614)
XLA Ops:
  0.6 59.3 %shard_map.67 = (f32[8,2304]{1,0:T(8,128)S(1)}, f32[1,8]{1,0:T(1,128)S(1)}, f32[18,128]{1,0:T(8,128)S(1)}) custom-call(bf16[1,8,73728]{2,1,0:T(8,128)(2,1)} %g_hbm.1, bf16[8,2304]{1,0:T(8,128)(2,1)} %w_hbm.1, f32[1,8]{1,0:T(1,128)} %bitcast.7, f32[18,128]{1,0:T(8,128)} %bitcast.6), custom_call_target="tpu_custom_call" | custom-call | tf_op jit(solution)/shard_map/pallas_call | solution.py:330
  59.9 0.6 %copy.10 = f32[8,2304]{1,0:T(8,128)} copy(f32[8,2304]{1,0:T(8,128)S(1)} %get-tuple-element.12) | data formatting | bytes 147456
  60.6 0.5 copy.11
  61.1 0.6 copy.12
